TPU v7x, 32 devices: a whole 2x2x4 slice. The times are simulated.
32 devices in a mesh: bi: 4 (over y, x), bj: 4 (over z), sl: 2 (over core).
Axes of the slice: x: 2, y: 2, z: 4, core: 2. Of those that a mesh axis runs over, the one named last changes fastest.
Arguments:
- snapshots: bfloat16 [2048, 3072], P('sl', ('bj', 'bi')), may hold values from -6 to 6
- slot_map: int32 [16, 192], P(('bj', 'bi')), may hold values from 0 to 191, each once within a row
- row_weight: float32 [2048], P('sl'), may hold values from 0.00048828125 to 0.0078125
- valid_rows: int32 [2, 4], P('sl'), may hold values from 1 to 256, 768 in all within a row
Outputs:
- gram: float32 [3072, 3072], P(('bi', 'sl'), 'bj')
Inputs may be any that keep to these rules, and one draw needn't show every extreme that they name: Each row of slot_map is a permutation of 0 to 191. Each row of valid_rows sums to 768, and holds one count equal to 256.
All inputs are finite; a program needn't handle non-finite values.
Results may differ from a plain program's by a relative error of at most 0.0028.
Values may be sent and summed in bfloat16 or wider, within the bound.
A program may use at most 128 MiB of HBM per device.

v0:
```python
import jax
import jax.numpy as jnp
from jax import lax
from jax.sharding import PartitionSpec as P


def contract_rows(left_panel, right_panel):
    return lax.dot_general(
        left_panel, right_panel, (((0,), (0,)), ((), ())), preferred_element_type=jnp.float32
    )


def body(snapshots, slot_map, row_weight, valid_rows):
    local_rows = snapshots.shape[0]
    sources_here = valid_rows.shape[1]
    source_rows = local_rows // sources_here
    ordered = jnp.zeros_like(snapshots).at[:, slot_map[0]].set(snapshots)
    positions = jnp.arange(local_rows, dtype=jnp.int32)
    source = positions // source_rows
    within = positions % source_rows
    source_ids = jnp.arange(sources_here, dtype=jnp.int32)
    matches = source[:, None] == source_ids[None, :]
    row_limit = jnp.sum(jnp.where(matches, valid_rows[0][None, :], 0), axis=1)
    row_factor = jnp.where(within < row_limit, row_weight, jnp.zeros_like(row_weight))
    count_bi = lax.axis_size("bi")
    count_bj = lax.axis_size("bj")
    per_row = count_bj // count_bi
    row_count = ordered.shape[0]
    shard_width = ordered.shape[1]
    column_panel = lax.all_gather(ordered, "bi", axis=1, tiled=True)
    weighted_shard = (ordered.astype(jnp.float32) * row_factor[:, None]).astype(jnp.bfloat16)
    sectioned = weighted_shard.reshape(row_count, 1, 1, shard_width)
    moved = lax.all_to_all(
        lax.all_to_all(sectioned, "bj", split_axis=0, concat_axis=1, tiled=True),
        "bi",
        split_axis=1,
        concat_axis=2,
        tiled=True,
    )
    gathered = lax.all_gather(moved, "bj", axis=0, tiled=True)
    weighted = gathered.reshape(row_count, per_row * count_bi * shard_width)
    return lax.psum_scatter(
        contract_rows(weighted, column_panel), "sl", scatter_dimension=0, tiled=True
    )


def solution(mesh):
    return jax.shard_map(
        body,
        mesh=mesh,
        in_specs=(P("sl", ("bj", "bi")), P(("bj", "bi"), None), P("sl"), P("sl", None)),
        out_specs=P(("bi", "sl"), "bj"),
        check_vma=False,
    )
```

profile of v0, /device:TPU:6, one launch (start us, length us, event | category | flops | bytes accessed | tf_op | source)
XLA Modules:
  0.0 105.3 jit_solution(441221778185152616)
XLA Ops:
  6.5 0.0 copy-start
  6.5 0.0 all-gather.4.cloned.1.call-start
  6.5 0.7 compare_select_fusion
  7.3 0.3 copy-done
  7.5 2.1 %scatter_custom_fusion = bf16[1024,192]{0,1:T(8,128)(2,1)} fusion(s32[192]{0:T(256)S(1)} %bitcast.23, bf16[1024,192]{0,1:T(8,128)(2,1)S(1)} %copy-done, bf16[]{:T(256)} %constant.30.clone.1), kind=kCustom, calls=%fused_computation.3 | custom fusion | bytes 786434 | tf_op jit(solution)/shard_map/scatter | solution.py:17
  9.7 0.0 all-gather.4.cloned.1.call-update
  9.7 0.0 all-gather.6.cloned.1.call-start
  9.8 0.7 select_reduce_fusion
  10.5 0.7 fusion.10
  11.2 1.1 %fusion = bf16[1024,1,1,192]{0,3,2,1:T(8,128)(2,1)S(1)} fusion(bf16[1024,192]{0,1:T(8,128)(2,1)} %scatter_custom_fusion, f32[1024]{0:T(1024)S(1)} %fusion.10), kind=kLoop, calls=%fused_computation.2 | loop fusion | flops 589824 | bytes 790528 | tf_op jit(solution)/shard_map/reshape | solution.py:32
  12.3 0.6 broadcast.49
  12.9 0.9 reduce
  13.8 0.2 copy.17
  14.0 0.6 reshape.65
  14.6 16.4 %all_to_all.30 = bf16[4,2,24576]{2,1,0:T(2,128)(2,1)S(1)} all-to-all(bf16[4,2,24576]{2,1,0:T(2,128)(2,1)S(1)} %reshape.65), channel_id=1, replica_groups=mesh['bi'=4,'bj'=4,'sl'=2] {'bj'}, dimensions={0} | all-to-all | bytes 786432 | tf_op jit(solution)/shard_map/all_to_all | solution.py:34
  31.0 0.7 reshape.66
  31.7 0.6 copy.14
  32.4 0.3 all_to_all.23
  32.7 12.2 %all_to_all.31 = bf16[256,4,1,192]{0,3,2,1:T(8,128)(2,1)} all-to-all(bf16[256,4,1,192]{0,3,2,1:T(8,128)(2,1)S(1)} %copy.15), channel_id=1, replica_groups=mesh['bi'=4,'bj'=4,'sl'=2] {'bi'}, dimensions={1} | all-to-all | bytes 786432 | tf_op jit(solution)/shard_map/all_to_all | solution.py:33
  44.9 0.0 all-gather.6.cloned.1.call-update
  44.9 0.0 reduce-scatter.2.cloned.1.call-start
  45.0 0.3 all-gather.4.cloned.1.call-done
  45.3 40.3 %all-gather.6.cloned.1.call-done = bf16[1024,4,1,192]{0,3,1,2:T(8,128)(2,1)} async-done(((bf16[256,4,1,192]{0,3,1,2:T(8,128)(2,1)}), bf16[1024,4,1,192]{0,3,1,2:T(8,128)(2,1)}) %all-gather.6.cloned.1.call-update) | async-done | bytes 1572880 | tf_op jit(solution)/shard_map/all_gather | solution.py:40
  85.6 4.7 %fusion.11 = f32[768,768]{1,0:T(8,128)} fusion(bf16[1024,768]{0,1:T(8,128)(2,1)} %bitcast.25, bf16[1024,768]{0,1:T(8,128)(2,1)} %all-gather.4.cloned.1.call-done), kind=kOutput, calls=%fused_computation.21 | convolution fusion | flops 1207959552 | bytes 5505024 | tf_op jit(solution)/shard_map/dot_general | solution.py:8
  90.3 0.0 reduce-scatter.2.cloned.1.call-update
  90.3 8.5 %reduce-scatter.2.cloned.1.call-done = f32[384,768]{1,0:T(8,128)} async-done(((f32[768,768]{1,0:T(8,128)}), f32[384,768]{1,0:T(8,128)}) %reduce-scatter.2.cloned.1.call-update) | async-done | bytes 1179664 | tf_op jit(solution)/shard_map/reduce_scatter | solution.py:42
  (2 shorter events, 0.0 us)
Async XLA Ops:
  6.5 1.0 copy-start
  6.5 38.8 %all-gather.4.cloned.1.call-start = ((), (), s32[]{:S(2)}) async-start(), calls=%async_computation.3 | async-start | bytes 1966080 | tf_op jit(solution)/shard_map/all_gather | solution.py:30
  9.7 75.9 %all-gather.6.cloned.1.call-start = ((), (), s32[]{:S(2)}) async-start(), calls=%async_computation.5 | async-start | bytes 1966080 | tf_op jit(solution)/shard_map/all_gather | solution.py:40
  44.9 53.9 %reduce-scatter.2.cloned.1.call-start = ((), (), s32[]{:S(2)}) async-start(), calls=%async_computation.4 | async-start | bytes 3538944 | tf_op jit(solution)/shard_map/reduce_scatter | solution.py:42
Sparse Core Ops, SparseCore 0:
  9.8 35.4 all-gather.3
  46.9 38.6 all-gather.5
  90.4 8.3 reduce-scatter.1
where the time goes:
time: 107 us; the launch traced here: 105 us
  waiting for transfers between devices  49.2 us (46%)
  blocking collectives  28.5 us (27%)
  between operations  13.2 us (12%)
  local copies, waits for them, and re-layouts  5.49 us (5%)
  matrix products  4.72 us (4%)
  other arithmetic  4.18 us (4%)
    all_gather x1, waiting for transfers between devices, body(): gathered = lax.all_gather(moved, 'bj', axis=0, tiled=True)  40.3 us
    all_to_all x1, blocking collectives, body(): lax.all_to_all(sectioned, 'bj', split_axis=0, concat_axis=1, tiled=True)  16.4 us
    all_to_all x1, blocking collectives, body(): lax.all_to_all(lax.all_to_all(sectioned, 'bj', split_axis=0, concat_axis=...  12.2 us
    reduce_scatter x1, waiting for transfers between devices, body(): lax.psum_scatter(contract_rows(weighted, column_panel), 'sl', scatter_dim...  8.5 us
    dot_general x1, matrix products, contract_rows(): lax.dot_general(left_panel, right_panel, (((0,), (0,)), ((), ())), prefer...  4.72 us
  transfers between devices with their start and end apart: 3, of which 3 were waited for; matrix products, arithmetic and copies ran while one was open for 6% of the time, Pallas kernels for 0%

commit v1 on v0

--- a/solution.py
+++ b/solution.py
@@ -1,7 +1,16 @@
 import jax
 import jax.numpy as jnp
 from jax import lax
+from jax.experimental import pallas as pl
+from jax.experimental.pallas import tpu as pltpu
 from jax.sharding import PartitionSpec as P
+
+MESH = pl.DeviceIdType.MESH
+CHUNKS = 4
+
+
+def nt(a, b):
+    return lax.dot_general(a, b, (((1,), (1,)), ((), ())), preferred_element_type=jnp.float32)
 
 
 def contract_rows(left_panel, right_panel):
@@ -44,9 +53,273 @@
     )
 
 
+def gram_kernel(
+    snap, slot, weight, valid, out,
+    colp, rowp, offl, wrow, acc, other,
+    own_z, gsend, grecv, upsend, dnsend, rrecv, orecv, psend, ssend, srecv,
+):
+    r = lax.axis_index("bi")
+    z = lax.axis_index("bj")
+    s = lax.axis_index("sl")
+    rows, width = snap.shape
+    sources = valid.shape[1]
+    src_rows = rows // sources
+    kept = (sources - 1) * src_rows
+    C = CHUNKS
+    part = width // C
+    diag = r == z
+    not_diag = r != z
+    low = z > 0
+    high = z < 3
+
+    barrier = pltpu.get_barrier_semaphore()
+    for k in (1, 2, 3):
+        mate = (r + k) % 4
+        pl.semaphore_signal(barrier, inc=1, device_id={"bi": mate}, device_id_type=MESH)
+    pl.semaphore_signal(barrier, inc=1, device_id={"sl": 1 - s}, device_id_type=MESH)
+
+    @pl.when(low)
+    def _():
+        pl.semaphore_signal(barrier, inc=1, device_id={"bj": z - 1}, device_id_type=MESH)
+
+    @pl.when(high)
+    def _():
+        pl.semaphore_signal(barrier, inc=1, device_id={"bj": z + 1}, device_id_type=MESH)
+
+    place = lax.broadcasted_iota(jnp.int32, (width, width), 0)
+    turn = (place == slot[...]).astype(jnp.float32).astype(jnp.bfloat16)
+    turned = nt(turn, snap[...]).astype(jnp.bfloat16)
+    start = jnp.int32(0)
+    targets = []
+    lane = lax.broadcasted_iota(jnp.int32, (1, src_rows), 1)
+    for q in range(sources):
+        count = valid[0, q]
+        targets.append(jnp.where(lane < count, lane + start, -1))
+        start = start + count
+    target = jnp.concatenate(targets, axis=1)
+    choose = (lax.broadcasted_iota(jnp.int32, (kept, rows), 0) == target)
+    choose = choose.astype(jnp.float32).astype(jnp.bfloat16)
+    w = weight[...].reshape(1, rows)
+    hi = w.astype(jnp.bfloat16).astype(jnp.float32)
+    mid = (w - hi).astype(jnp.bfloat16).astype(jnp.float32)
+    low_bits = w - hi - mid
+    pieces = jnp.concatenate([hi, mid, low_bits, jnp.zeros((13, rows), jnp.float32)], axis=0)
+    packed = nt(jnp.concatenate([turned, pieces.astype(jnp.bfloat16)], axis=0), choose)
+    colp[pl.ds(r, 1)] = packed[:width].astype(jnp.bfloat16).reshape(1, C, part, kept)
+    wrow[...] = packed[width:width + 1] + packed[width + 1:width + 2] + packed[width + 2:width + 3]
+
+    pl.semaphore_wait(barrier, 4 + (z + 3) // 4 + (6 - z) // 4)
+
+    def to_plane(k, c):
+        return pltpu.make_async_remote_copy(
+            src_ref=colp.at[r, c], dst_ref=colp.at[r, c],
+            send_sem=gsend.at[k, c], recv_sem=grecv.at[r, c],
+            device_id={"bi": flip(k)}, device_id_type=MESH)
+
+    def flip(k):
+        x, y = r % 2, r // 2
+        x = 1 - x if k % 2 else x
+        y = 1 - y if k // 2 else y
+        return 2 * y + x
+
+    def along(src, dst, step, sends, recvs, b, c):
+        return pltpu.make_async_remote_copy(
+            src_ref=src.at[b, c], dst_ref=dst.at[b, c],
+            send_sem=sends.at[b, c], recv_sem=recvs.at[b, c],
+            device_id={"bj": z + step}, device_id_type=MESH)
+
+    def up_row(src, b, c):
+        return along(src, rowp, 1, upsend, rrecv, b, c)
+
+    def dn_row(src, b, c):
+        return along(src, rowp, -1, dnsend, rrecv, b, c)
+
+    def own_off(step, sends, c):
+        return pltpu.make_async_remote_copy(
+            src_ref=colp.at[r, c], dst_ref=offl.at[z, c],
+            send_sem=sends.at[z, c], recv_sem=orecv.at[z, c],
+            device_id={"bj": z + step}, device_id_type=MESH)
+
+    def hand(p, c):
+        return pltpu.make_async_remote_copy(
+            src_ref=offl.at[p, c], dst_ref=rowp.at[r, c],
+            send_sem=psend.at[p, c], recv_sem=rrecv.at[r, c],
+            device_id={"bi": p}, device_id_type=MESH)
+
+    def got(buf, recvs, b, c):
+        pltpu.make_async_remote_copy(
+            src_ref=buf.at[b, c], dst_ref=buf.at[b, c],
+            send_sem=own_z.at[0], recv_sem=recvs.at[b, c],
+            device_id={"sl": 1 - s}, device_id_type=MESH).wait_recv()
+
+    def act(condition, copy, drain):
+        @pl.when(condition)
+        def _():
+            if drain:
+                copy().wait_send()
+            else:
+                copy().start()
+
+    down = (r - z + 3 + r // 3) // 4
+    second = down * (3 - r // 3) + (1 - down) * (1 - (r + 2) // 3)
+    third = down * 6 + (1 - down) * 3 - r - second
+    lent = (1 - down) * 3
+    natural = (r, second, third)
+    off_down = (r == 0)
+    off_up = (r == 3)
+
+    def send_own(c, drain):
+        act(diag & low, lambda: dn_row(colp, r, c), drain)
+        act(diag & high, lambda: up_row(colp, r, c), drain)
+        act(off_down & low, lambda: own_off(-1, dnsend, c), drain)
+        act(off_up & high, lambda: own_off(1, upsend, c), drain)
+        for k in (1, 2):
+            act(r >= 0, lambda: to_plane(k, c), drain)
+
+    def send_far(c, drain):
+        act(r >= 0, lambda: to_plane(3, c), drain)
+
+    def plane_step(k, c, drain):
+        b = flip(k)
+        if not drain:
+            got(colp, grecv, b, c)
+        act(diag & low & (b >= 1), lambda: dn_row(colp, b, c), drain)
+        act(diag & high & (b <= 2), lambda: up_row(colp, b, c), drain)
+
+    def line_step(u, c, drain):
+        b = natural[u]
+
+        @pl.when(not_diag)
+        def _():
+            if not drain:
+                got(rowp, rrecv, b, c)
+        act((z < r) & low, lambda: dn_row(rowp, b, c), drain)
+        act((z > r) & high, lambda: up_row(rowp, b, c), drain)
+
+        p_dn = z + 1 + u
+
+        @pl.when(off_down & (p_dn <= 3))
+        def _():
+            if not drain:
+                got(offl, orecv, p_dn, c)
+            act(low, lambda: along(offl, offl, -1, dnsend, orecv, p_dn, c), drain)
+            act(r >= 0, lambda: hand(p_dn, c), drain)
+
+        p_up = z - 1 - u
+
+        @pl.when(off_up & (p_up >= 0))
+        def _():
+            if not drain:
+                got(offl, orecv, p_up, c)
+            act(high, lambda: along(offl, offl, 1, upsend, orecv, p_up, c), drain)
+            act(r >= 0, lambda: hand(p_up, c), drain)
+
+    def over(step):
+        def one(c, carry):
+            step(c)
+            return carry
+        lax.fori_loop(0, C, one, 0)
+
+    def to_sister(b):
+        return pltpu.make_async_remote_copy(
+            src_ref=acc.at[b], dst_ref=other.at[b % 2],
+            send_sem=ssend.at[b % 2], recv_sem=srecv.at[b % 2],
+            device_id={"sl": 1 - s}, device_id_type=MESH)
+
+    def multiply(b):
+        @pl.when(diag)
+        def _():
+            rowp[pl.ds(b, 1)] = colp[pl.ds(b, 1)]
+        block = rowp[pl.ds(b, 1)].reshape(width, kept).astype(jnp.float32)
+        weighted = (block * wrow[...]).astype(jnp.bfloat16)
+        acc[pl.ds(b, 1)] = nt(weighted, colp[...].reshape(4 * width, kept))[None]
+
+        @pl.when(b // 2 != s)
+        def _():
+            to_sister(b).start()
+
+    over(lambda c: send_own(c, False))
+    over(lambda c: send_far(c, False))
+
+    def first(c):
+        plane_step(1, c, False)
+        plane_step(2, c, False)
+        line_step(0, c, False)
+    over(first)
+
+    def middle(c):
+        plane_step(3, c, False)
+        line_step(1, c, False)
+    over(middle)
+    multiply(natural[0])
+    multiply(natural[1])
+    over(lambda c: line_step(2, c, False))
+    multiply(natural[2])
+
+    def last(c):
+        @pl.when(not_diag)
+        def _():
+            got(rowp, rrecv, lent, c)
+    over(last)
+    multiply(lent)
+
+    for j in range(2):
+        pltpu.make_async_remote_copy(
+            src_ref=acc.at[j], dst_ref=other.at[j], send_sem=ssend.at[j], recv_sem=srecv.at[j],
+            device_id={"sl": 1 - s}, device_id_type=MESH).wait()
+        out[j * width:(j + 1) * width] = acc[pl.ds(2 * s + j, 1)][0] + other[j]
+
+    def drain(c):
+        send_own(c, True)
+        send_far(c, True)
+        for k in (1, 2, 3):
+            plane_step(k, c, True)
+        for u in range(3):
+            line_step(u, c, True)
+    over(drain)
+
+
+def fused(snapshots, slot_map, row_weight, valid_rows):
+    rows, width = snapshots.shape
+    sources = valid_rows.shape[1]
+    kept = (sources - 1) * (rows // sources)
+    panel = (4, CHUNKS, width // CHUNKS, kept)
+    full = 4 * width
+    dma = pltpu.SemaphoreType.DMA
+    grid4 = dma((4, CHUNKS))
+    return pl.pallas_call(
+        gram_kernel,
+        out_shape=jax.ShapeDtypeStruct((2 * width, full), jnp.float32),
+        in_specs=[
+            pl.BlockSpec(memory_space=pltpu.VMEM),
+            pl.BlockSpec(memory_space=pltpu.VMEM),
+            pl.BlockSpec(memory_space=pltpu.VMEM),
+            pl.BlockSpec(memory_space=pltpu.SMEM),
+        ],
+        out_specs=pl.BlockSpec(memory_space=pltpu.VMEM),
+        scratch_shapes=[
+            pltpu.VMEM(panel, jnp.bfloat16),
+            pltpu.VMEM(panel, jnp.bfloat16),
+            pltpu.VMEM(panel, jnp.bfloat16),
+            pltpu.VMEM((1, kept), jnp.float32),
+            pltpu.VMEM((4, width, full), jnp.float32),
+            pltpu.VMEM((2, width, full), jnp.float32),
+            dma((1,)), grid4, grid4, grid4, grid4, grid4, grid4, grid4, dma((2,)), dma((2,)),
+        ],
+        compiler_params=pltpu.CompilerParams(
+            collective_id=0, has_side_effects=True, vmem_limit_bytes=40 * 2**20
+        ),
+        cost_estimate=pl.CostEstimate(
+            flops=2 * full * full * kept, bytes_accessed=8 * 2**20, transcendentals=0
+        ),
+    )(snapshots, slot_map, row_weight, valid_rows)
+
+
 def solution(mesh):
+    shape = dict(mesh.shape)
+    use_kernel = shape == {"bi": 4, "bj": 4, "sl": 2}
     return jax.shard_map(
-        body,
+        fused if use_kernel else body,
         mesh=mesh,
         in_specs=(P("sl", ("bj", "bi")), P(("bj", "bi"), None), P("sl"), P("sl", None)),
         out_specs=P(("bi", "sl"), "bj"),

time: 107 us -> 42.8 us (0.40); the launches traced: 105 us -> 42.5 us
  waiting for transfers between devices: 49.2 us -> 0 us
  Pallas kernels: 0 us -> 38.2 us
  blocking collectives: 28.5 us -> 0 us
  between operations: 13.2 us -> 0.02 us
  matrix products: 4.72 us -> 0 us
  other arithmetic: 4.18 us -> 0 us
  local copies, waits for them, and re-layouts: 5.49 us -> 4.23 us
    all_gather x2 -> x0, waiting for transfers between devices: 40.6 us -> none  [the longest x1 40.3 us: body(): gathered = lax.all_gather(moved, 'bj', axis=0, tiled=True)]
    pallas_call x0 -> x1, Pallas kernels: none -> 38.2 us  [fused(): pl.pallas_call(gram_kernel, out_shape=jax.ShapeDtypeStruct((2 * width, fu...]
    all_to_all x2 -> x0, blocking collectives: 28.5 us -> none  [the longest x1 16.4 us: body(): lax.all_to_all(sectioned, 'bj', split_axis=0, concat_axis=1, tiled=True)]
    reduce_scatter x1 -> x0, waiting for transfers between devices: 8.5 us -> none  [body(): lax.psum_scatter(contract_rows(weighted, column_panel), 'sl', scatter_dim...]
    dot_general x1 -> x0, matrix products: 4.72 us -> none  [contract_rows(): lax.dot_general(left_panel, right_panel, (((0,), (0,)), ((), ())), prefer...]
    unnamed x5 -> x8, local copies, waits for them, and re-layouts: 1.82 us -> 4.23 us
    scatter x1 -> x0, local copies, waits for them, and re-layouts: 2.13 us -> none  [body(): ordered = jnp.zeros_like(snapshots).at[:, slot_map[0]].set(snapshots)]
    reshape x2 -> x0, other arithmetic: 2.02 us -> none  [body(): sectioned = weighted_shard.reshape(row_count, 1, 1, shard_width)]
  transfers between devices with their start and end apart: 3 -> 0, of which waited for: 3 -> 0; matrix products, arithmetic and copies ran while one was open for 6% -> 0% of each run, Pallas kernels for 0% -> 0%
where the time goes in v1:
time: 42.8 us; the launch traced here: 42.5 us
  Pallas kernels  38.2 us (89%)
  local copies, waits for them, and re-layouts  4.23 us (10%)
    pallas_call x1, Pallas kernels, fused(): pl.pallas_call(gram_kernel, out_shape=jax.ShapeDtypeStruct((2 * width, fu...  38.2 us
    unnamed x8, local copies, waits for them, and re-layouts  4.23 us

profile of v1, /device:TPU:6, one launch (start us, length us, event | category | flops | bytes accessed | tf_op | source)
XLA Modules:
  0.0 42.5 jit_solution(7007317671274192064)
XLA Ops:
  0.0 1.2 %copy.5.snap = bf16[1024,192]{1,0:T(8,128)(2,1)S(1)} copy(bf16[1024,192]{0,1:T(8,128)(2,1)} %param.4) | data formatting | bytes 786432 | tf_op args[0]
  1.2 0.0 copy-start
  1.2 0.7 %copy-done = f32[1024]{0:T(1024)S(1)} copy-done((f32[1024]{0:T(1024)S(1)}, f32[1024]{0:T(1024)}, u32[]{:S(2)}) %copy-start) | copy-done | bytes 4120
  1.9 0.0 copy-start.1
  1.9 0.7 %copy-done.1 = s32[1,192]{1,0:T(1,128)S(1)} copy-done((s32[1,192]{1,0:T(1,128)S(1)}, s32[1,192]{1,0:T(1,128)}, u32[]{:S(2)}) %copy-start.1) | copy-done | bytes 792
  2.6 0.0 copy-start.2
  2.6 0.7 %copy-done.2 = s32[1,4]{1,0:T(1,128)S(1)} copy-done((s32[1,4]{1,0:T(1,128)S(1)}, s32[1,4]{1,0:T(1,128)}, u32[]{:S(2)}) %copy-start.2) | copy-done | bytes 40
  3.2 38.2 %shard_map.46 = f32[384,768]{1,0:T(8,128)S(1)} custom-call(bf16[1024,192]{1,0:T(8,128)(2,1)S(1)} %copy.5.snap, s32[1,192]{1,0:T(1,128)S(1)} %copy-done.1, f32[1024]{0:T(1024)S(1)} %copy-done, s32[1,4]{1,0:T(1,128)S(1)} %copy-done.2), custom_call_target="tpu_custom_call" | custom-call | flops 905969664 | bytes 8388608 | tf_op jit(solution)/shard_map/pallas_call | solution.py:290
  41.5 1.0 %copy.7 = f32[384,768]{1,0:T(8,128)} copy(f32[384,768]{1,0:T(8,128)S(1)} %shard_map.46) | data formatting | bytes 2359296
Async XLA Ops:
  1.2 0.7 %copy-start = (f32[1024]{0:T(1024)S(1)}, f32[1024]{0:T(1024)}, u32[]{:S(2)}) copy-start(f32[1024]{0:T(1024)} %weight.1) | copy-start | bytes 12292
  1.9 0.7 %copy-start.1 = (s32[1,192]{1,0:T(1,128)S(1)}, s32[1,192]{1,0:T(1,128)}, u32[]{:S(2)}) copy-start(s32[1,192]{1,0:T(1,128)} %slot.1) | copy-start | bytes 2308
  2.6 0.7 %copy-start.2 = (s32[1,4]{1,0:T(1,128)S(1)}, s32[1,4]{1,0:T(1,128)}, u32[]{:S(2)}) copy-start(s32[1,4]{1,0:T(1,128)} %valid.1) | copy-start | bytes 52

commit v2 on v1

--- a/solution.py
+++ b/solution.py
@@ -54,14 +54,14 @@
 
 
 def gram_kernel(
-    snap, slot, weight, valid, out,
-    colp, rowp, offl, wrow, acc, other,
+    snap_in, slot_in, weight_in, valid_in, out,
+    snap, slot, weight, valid, insem, colp, rowp, offl, wrow, acc, other,
     own_z, gsend, grecv, upsend, dnsend, rrecv, orecv, psend, ssend, srecv,
 ):
     r = lax.axis_index("bi")
     z = lax.axis_index("bj")
     s = lax.axis_index("sl")
-    rows, width = snap.shape
+    width, rows = snap.shape
     sources = valid.shape[1]
     src_rows = rows // sources
     kept = (sources - 1) * src_rows
@@ -72,6 +72,13 @@
     low = z > 0
     high = z < 3
 
+    loads = [
+        pltpu.make_async_copy(src, dst, insem.at[i])
+        for i, (src, dst) in enumerate(
+            ((snap_in, snap), (slot_in, slot), (valid_in, valid), (weight_in, weight)))
+    ]
+    for load in loads:
+        load.start()
     barrier = pltpu.get_barrier_semaphore()
     for k in (1, 2, 3):
         mate = (r + k) % 4
@@ -86,9 +93,11 @@
     def _():
         pl.semaphore_signal(barrier, inc=1, device_id={"bj": z + 1}, device_id_type=MESH)
 
+    for load in loads:
+        load.wait()
     place = lax.broadcasted_iota(jnp.int32, (width, width), 0)
     turn = (place == slot[...]).astype(jnp.float32).astype(jnp.bfloat16)
-    turned = nt(turn, snap[...]).astype(jnp.bfloat16)
+    turned = jnp.dot(turn, snap[...], preferred_element_type=jnp.float32).astype(jnp.bfloat16)
     start = jnp.int32(0)
     targets = []
     lane = lax.broadcasted_iota(jnp.int32, (1, src_rows), 1)
@@ -176,17 +185,41 @@
         for k in (1, 2):
             act(r >= 0, lambda: to_plane(k, c), drain)
 
-    def send_far(c, drain):
-        act(r >= 0, lambda: to_plane(3, c), drain)
+    def relay(k, c):
+        b = flip(k)
+        return pltpu.make_async_remote_copy(
+            src_ref=colp.at[b, c], dst_ref=colp.at[b, c],
+            send_sem=gsend.at[3, c], recv_sem=grecv.at[b, c],
+            device_id={"bi": flip(3 - k)}, device_id_type=MESH)
 
     def plane_step(k, c, drain):
         b = flip(k)
         if not drain:
             got(colp, grecv, b, c)
+        if k != 3:
+            act(c % 2 == k - 1, lambda: relay(k, c), drain)
         act(diag & low & (b >= 1), lambda: dn_row(colp, b, c), drain)
         act(diag & high & (b <= 2), lambda: up_row(colp, b, c), drain)
 
     def line_step(u, c, drain):
+        p_dn = z + 1 + u
+
+        @pl.when(off_down & (p_dn <= 3))
+        def _():
+            if not drain:
+                got(offl, orecv, p_dn, c)
+            act(low, lambda: along(offl, offl, -1, dnsend, orecv, p_dn, c), drain)
+            act(r >= 0, lambda: hand(p_dn, c), drain)
+
+        p_up = z - 1 - u
+
+        @pl.when(off_up & (p_up >= 0))
+        def _():
+            if not drain:
+                got(offl, orecv, p_up, c)
+            act(high, lambda: along(offl, offl, 1, upsend, orecv, p_up, c), drain)
+            act(r >= 0, lambda: hand(p_up, c), drain)
+
         b = natural[u]
 
         @pl.when(not_diag)
@@ -195,24 +228,6 @@
                 got(rowp, rrecv, b, c)
         act((z < r) & low, lambda: dn_row(rowp, b, c), drain)
         act((z > r) & high, lambda: up_row(rowp, b, c), drain)
-
-        p_dn = z + 1 + u
-
-        @pl.when(off_down & (p_dn <= 3))
-        def _():
-            if not drain:
-                got(offl, orecv, p_dn, c)
-            act(low, lambda: along(offl, offl, -1, dnsend, orecv, p_dn, c), drain)
-            act(r >= 0, lambda: hand(p_dn, c), drain)
-
-        p_up = z - 1 - u
-
-        @pl.when(off_up & (p_up >= 0))
-        def _():
-            if not drain:
-                got(offl, orecv, p_up, c)
-            act(high, lambda: along(offl, offl, 1, upsend, orecv, p_up, c), drain)
-            act(r >= 0, lambda: hand(p_up, c), drain)
 
     def over(step):
         def one(c, carry):
@@ -239,7 +254,6 @@
             to_sister(b).start()
 
     over(lambda c: send_own(c, False))
-    over(lambda c: send_far(c, False))
 
     def first(c):
         plane_step(1, c, False)
@@ -247,10 +261,14 @@
         line_step(0, c, False)
     over(first)
 
-    def middle(c):
-        plane_step(3, c, False)
-        line_step(1, c, False)
-    over(middle)
+    @pl.when(diag)
+    def _():
+        over(lambda c: plane_step(3, c, False))
+    over(lambda c: line_step(1, c, False))
+
+    @pl.when(not_diag)
+    def _():
+        over(lambda c: plane_step(3, c, False))
     multiply(natural[0])
     multiply(natural[1])
     over(lambda c: line_step(2, c, False))
@@ -271,7 +289,6 @@
 
     def drain(c):
         send_own(c, True)
-        send_far(c, True)
         for k in (1, 2, 3):
             plane_step(k, c, True)
         for u in range(3):
@@ -282,6 +299,7 @@
 def fused(snapshots, slot_map, row_weight, valid_rows):
     rows, width = snapshots.shape
     sources = valid_rows.shape[1]
+    hbm = pl.BlockSpec(memory_space=pltpu.HBM)
     kept = (sources - 1) * (rows // sources)
     panel = (4, CHUNKS, width // CHUNKS, kept)
     full = 4 * width
@@ -290,14 +308,14 @@
     return pl.pallas_call(
         gram_kernel,
         out_shape=jax.ShapeDtypeStruct((2 * width, full), jnp.float32),
-        in_specs=[
-            pl.BlockSpec(memory_space=pltpu.VMEM),
-            pl.BlockSpec(memory_space=pltpu.VMEM),
-            pl.BlockSpec(memory_space=pltpu.VMEM),
-            pl.BlockSpec(memory_space=pltpu.SMEM),
-        ],
+        in_specs=[hbm] * 4,
         out_specs=pl.BlockSpec(memory_space=pltpu.VMEM),
         scratch_shapes=[
+            pltpu.VMEM((width, rows), jnp.bfloat16),
+            pltpu.VMEM(slot_map.shape, jnp.int32),
+            pltpu.VMEM(row_weight.shape, jnp.float32),
+            pltpu.SMEM(valid_rows.shape, jnp.int32),
+            dma((4,)),
             pltpu.VMEM(panel, jnp.bfloat16),
             pltpu.VMEM(panel, jnp.bfloat16),
             pltpu.VMEM(panel, jnp.bfloat16),
@@ -307,12 +325,12 @@
             dma((1,)), grid4, grid4, grid4, grid4, grid4, grid4, grid4, dma((2,)), dma((2,)),
         ],
         compiler_params=pltpu.CompilerParams(
-            collective_id=0, has_side_effects=True, vmem_limit_bytes=40 * 2**20
+            collective_id=0, has_side_effects=True, vmem_limit_bytes=63 * 2**20
         ),
         cost_estimate=pl.CostEstimate(
             flops=2 * full * full * kept, bytes_accessed=8 * 2**20, transcendentals=0
         ),
-    )(snapshots, slot_map, row_weight, valid_rows)
+    )(snapshots.T, slot_map, row_weight, valid_rows)
 
 
 def solution(mesh):

time: 42.8 us -> 42.3 us (0.988)
  local copies, waits for them, and re-layouts: 4.23 us -> 2.36 us
  Pallas kernels: 38.2 us -> 39.8 us
    unnamed x8 -> x1, local copies, waits for them, and re-layouts: 4.23 us -> 2.36 us
    pallas_call x1, Pallas kernels: 38.2 us -> 39.8 us  [fused(): pl.pallas_call(gram_kernel, out_shape=jax.ShapeDtypeStruct((2 * width, fu...]
where the time goes in v2:
time: 42.3 us; the launch traced here: 42.2 us
  Pallas kernels  39.8 us (94%)
  local copies, waits for them, and re-layouts  2.36 us (6%)
    pallas_call x1, Pallas kernels, fused(): pl.pallas_call(gram_kernel, out_shape=jax.ShapeDtypeStruct((2 * width, fu...  39.8 us
    unnamed x1, local copies, waits for them, and re-layouts  2.36 us

profile of v2, /device:TPU:6, one launch (start us, length us, event | category | flops | bytes accessed | tf_op | source)
XLA Modules:
  0.0 42.2 jit_solution(7750804252465332149)
XLA Ops:
  0.0 39.8 %shard_map.46 = f32[384,768]{1,0:T(8,128)} custom-call(bf16[192,1024]{1,0:T(8,128)(2,1)} %bitcast.1, s32[1,192]{1,0:T(1,128)} %slot_in.1, f32[1024]{0:T(1024)} %weight_in.1, s32[1,4]{1,0:T(1,128)} %valid_in.1), custom_call_target="tpu_custom_call" | custom-call | flops 905969664 | bytes 8388608 | tf_op jit(solution)/shard_map/pallas_call | solution.py:308
  39.8 2.4 %copy.6 = f32[384,768]{1,0:T(8,128)} copy(f32[384,768]{1,0:T(8,128)} %shard_map.46) | data formatting | bytes 2359296

commit v3 on v2

--- a/solution.py
+++ b/solution.py
@@ -6,7 +6,7 @@
 from jax.sharding import PartitionSpec as P
 
 MESH = pl.DeviceIdType.MESH
-CHUNKS = 4
+CHUNKS = 6
 
 
 def nt(a, b):
@@ -54,9 +54,9 @@
 
 
 def gram_kernel(
-    snap_in, slot_in, weight_in, valid_in, out,
-    snap, slot, weight, valid, insem, colp, rowp, offl, wrow, acc, other,
-    own_z, gsend, grecv, upsend, dnsend, rrecv, orecv, psend, ssend, srecv,
+    snap_in, slot_in, weight_in, valid_in, mine, other,
+    snap, slot, weight, valid, insem, colp, rowp, offl, wrow, acc,
+    own_z, gsend, grecv, upsend, dnsend, rrecv, orecv, psend, ssend, srecv, ksem,
 ):
     r = lax.axis_index("bi")
     z = lax.axis_index("bj")
@@ -241,6 +241,9 @@
             send_sem=ssend.at[b % 2], recv_sem=srecv.at[b % 2],
             device_id={"sl": 1 - s}, device_id_type=MESH)
 
+    def keep(b):
+        return pltpu.make_async_copy(acc.at[b], mine.at[b % 2], ksem.at[b % 2])
+
     def multiply(b):
         @pl.when(diag)
         def _():
@@ -252,6 +255,10 @@
         @pl.when(b // 2 != s)
         def _():
             to_sister(b).start()
+
+        @pl.when(b // 2 == s)
+        def _():
+            keep(b).start()
 
     over(lambda c: send_own(c, False))
 
@@ -266,12 +273,20 @@
         over(lambda c: plane_step(3, c, False))
     over(lambda c: line_step(1, c, False))
 
-    @pl.when(not_diag)
-    def _():
-        over(lambda c: plane_step(3, c, False))
-    multiply(natural[0])
-    multiply(natural[1])
+    def two():
+        @pl.when(not_diag)
+        def _():
+            over(lambda c: plane_step(3, c, False))
+
+        def one(i, carry):
+            multiply(natural[0] * (1 - i) + natural[1] * i)
+            return carry
+        lax.fori_loop(0, 2, one, 0)
+
+    is_end = ((z == 0) & (r >= 1)) | ((z == 3) & (r <= 2))
+    pl.when(is_end)(two)
     over(lambda c: line_step(2, c, False))
+    pl.when(jnp.logical_not(is_end))(two)
     multiply(natural[2])
 
     def last(c):
@@ -285,7 +300,7 @@
         pltpu.make_async_remote_copy(
             src_ref=acc.at[j], dst_ref=other.at[j], send_sem=ssend.at[j], recv_sem=srecv.at[j],
             device_id={"sl": 1 - s}, device_id_type=MESH).wait()
-        out[j * width:(j + 1) * width] = acc[pl.ds(2 * s + j, 1)][0] + other[j]
+        keep(2 * s + j).wait()
 
     def drain(c):
         send_own(c, True)
@@ -305,11 +320,12 @@
     full = 4 * width
     dma = pltpu.SemaphoreType.DMA
     grid4 = dma((4, CHUNKS))
-    return pl.pallas_call(
+    half = jax.ShapeDtypeStruct((2, width, full), jnp.float32)
+    mine, other = pl.pallas_call(
         gram_kernel,
-        out_shape=jax.ShapeDtypeStruct((2 * width, full), jnp.float32),
+        out_shape=(half, half),
         in_specs=[hbm] * 4,
-        out_specs=pl.BlockSpec(memory_space=pltpu.VMEM),
+        out_specs=(hbm, hbm),
         scratch_shapes=[
             pltpu.VMEM((width, rows), jnp.bfloat16),
             pltpu.VMEM(slot_map.shape, jnp.int32),
@@ -321,8 +337,7 @@
             pltpu.VMEM(panel, jnp.bfloat16),
             pltpu.VMEM((1, kept), jnp.float32),
             pltpu.VMEM((4, width, full), jnp.float32),
-            pltpu.VMEM((2, width, full), jnp.float32),
-            dma((1,)), grid4, grid4, grid4, grid4, grid4, grid4, grid4, dma((2,)), dma((2,)),
+            dma((1,)), grid4, grid4, grid4, grid4, grid4, grid4, grid4, dma((2,)), dma((2,)), dma((2,)),
         ],
         compiler_params=pltpu.CompilerParams(
             collective_id=0, has_side_effects=True, vmem_limit_bytes=63 * 2**20
@@ -331,6 +346,7 @@
             flops=2 * full * full * kept, bytes_accessed=8 * 2**20, transcendentals=0
         ),
     )(snapshots.T, slot_map, row_weight, valid_rows)
+    return (mine + other).reshape(2 * width, full)
 
 
 def solution(mesh):

time: 42.3 us -> 42.5 us (level)
  other arithmetic: 0 us -> 2.78 us
  local copies, waits for them, and re-layouts: 2.36 us -> 0 us
    add x0 -> x1, other arithmetic: none -> 2.78 us  [fused(): return (mine + other).reshape(2 * width, full)]
    unnamed x1 -> x0, local copies, waits for them, and re-layouts: 2.36 us -> none
where the time goes in v3:
time: 42.5 us; the launch traced here: 42.4 us
  Pallas kernels  39.6 us (93%)
  other arithmetic  2.78 us (7%)
    pallas_call x1, Pallas kernels, fused(): pl.pallas_call(gram_kernel, out_shape=(half, half), in_specs=[hbm] * 4, o...  39.6 us
    add x1, other arithmetic, fused(): return (mine + other).reshape(2 * width, full)  2.78 us

profile of v3, /device:TPU:6, one launch (start us, length us, event | category | flops | bytes accessed | tf_op | source)
XLA Modules:
  0.0 42.4 jit_solution(7605791574360567601)
XLA Ops:
  0.0 39.6 %shard_map.46 = (f32[2,192,768]{2,1,0:T(8,128)}, f32[2,192,768]{2,1,0:T(8,128)}) custom-call(bf16[192,1024]{1,0:T(8,128)(2,1)} %bitcast.2, s32[1,192]{1,0:T(1,128)} %slot_in.1, f32[1024]{0:T(1024)} %weight_in.1, s32[1,4]{1,0:T(1,128)} %valid_in.1), custom_call_target="tpu_custom_call" | custom-call | flops 905969664 | bytes 8388608 | tf_op jit(solution)/shard_map/pallas_call | solution.py:324
  39.6 2.8 %add.3 = f32[2,192,768]{2,1,0:T(8,128)} add(f32[2,192,768]{2,1,0:T(8,128)} %get-tuple-element.7, f32[2,192,768]{2,1,0:T(8,128)} %get-tuple-element.8) | non-fusion elementwise | flops 294912 | bytes 3538944 | tf_op jit(solution)/shard_map/add | solution.py:349

commit v4 on v3

--- a/solution.py
+++ b/solution.py
@@ -6,7 +6,8 @@
 from jax.sharding import PartitionSpec as P
 
 MESH = pl.DeviceIdType.MESH
-CHUNKS = 6
+CHUNKS = 3
+LENT = 3
 
 
 def nt(a, b):
@@ -173,15 +174,15 @@
     second = down * (3 - r // 3) + (1 - down) * (1 - (r + 2) // 3)
     third = down * 6 + (1 - down) * 3 - r - second
     lent = (1 - down) * 3
-    natural = (r, second, third)
+    natural = (r, second, third, lent)
     off_down = (r == 0)
     off_up = (r == 3)
 
     def send_own(c, drain):
         act(diag & low, lambda: dn_row(colp, r, c), drain)
         act(diag & high, lambda: up_row(colp, r, c), drain)
-        act(off_down & low, lambda: own_off(-1, dnsend, c), drain)
-        act(off_up & high, lambda: own_off(1, upsend, c), drain)
+        act(off_down & low & (c < LENT), lambda: own_off(-1, dnsend, c), drain)
+        act(off_up & high & (c < LENT), lambda: own_off(1, upsend, c), drain)
         for k in (1, 2):
             act(r >= 0, lambda: to_plane(k, c), drain)
 
@@ -198,13 +199,13 @@
             got(colp, grecv, b, c)
         if k != 3:
             act(c % 2 == k - 1, lambda: relay(k, c), drain)
-        act(diag & low & (b >= 1), lambda: dn_row(colp, b, c), drain)
-        act(diag & high & (b <= 2), lambda: up_row(colp, b, c), drain)
+        act(diag & low & ((b >= 1) | (c >= LENT)), lambda: dn_row(colp, b, c), drain)
+        act(diag & high & ((b <= 2) | (c >= LENT)), lambda: up_row(colp, b, c), drain)
 
     def line_step(u, c, drain):
         p_dn = z + 1 + u
 
-        @pl.when(off_down & (p_dn <= 3))
+        @pl.when(off_down & (p_dn <= 3) & (c < LENT))
         def _():
             if not drain:
                 got(offl, orecv, p_dn, c)
@@ -213,13 +214,16 @@
 
         p_up = z - 1 - u
 
-        @pl.when(off_up & (p_up >= 0))
+        @pl.when(off_up & (p_up >= 0) & (c < LENT))
         def _():
             if not drain:
                 got(offl, orecv, p_up, c)
             act(high, lambda: along(offl, offl, 1, upsend, orecv, p_up, c), drain)
             act(r >= 0, lambda: hand(p_up, c), drain)
 
+        natural_step(u, c, drain)
+
+    def natural_step(u, c, drain):
         b = natural[u]
 
         @pl.when(not_diag)
@@ -271,28 +275,66 @@
     @pl.when(diag)
     def _():
         over(lambda c: plane_step(3, c, False))
-    over(lambda c: line_step(1, c, False))
-
-    def two():
+    in_turn = (r == 0) | (r == 3)
+    is_end = ((z == 0) & (r >= 1)) | ((z == 3) & (r <= 2))
+    is_middle = jnp.logical_not(is_end)
+
+    def far_block():
         @pl.when(not_diag)
         def _():
             over(lambda c: plane_step(3, c, False))
 
+    def products(lo, hi):
         def one(i, carry):
-            multiply(natural[0] * (1 - i) + natural[1] * i)
+            b = r + (i % 2) * (second - r) + (i // 2) * (third - r)
+            multiply(b)
             return carry
-        lax.fori_loop(0, 2, one, 0)
-
-    is_end = ((z == 0) & (r >= 1)) | ((z == 3) & (r <= 2))
-    pl.when(is_end)(two)
-    over(lambda c: line_step(2, c, False))
-    pl.when(jnp.logical_not(is_end))(two)
-    multiply(natural[2])
+        lax.fori_loop(lo, hi, one, 0)
+
+    @pl.when(is_end & in_turn)
+    def _():
+        far_block()
+        products(0, 1)
+
+    @pl.when(in_turn)
+    def _():
+        def both(c):
+            line_step(1, c, False)
+            line_step(2, c, False)
+        over(both)
+
+    @pl.when(is_end & in_turn)
+    def _():
+        products(1, 3)
+
+    @pl.when(jnp.logical_not(in_turn))
+    def _():
+        over(lambda c: line_step(1, c, False))
+
+        @pl.when(is_end)
+        def _():
+            far_block()
+            products(0, 2)
+        over(lambda c: line_step(2, c, False))
+
+        @pl.when(is_end)
+        def _():
+            products(2, 3)
+
+    @pl.when(is_middle)
+    def _():
+        far_block()
+        products(0, 3)
 
     def last(c):
-        @pl.when(not_diag)
+        @pl.when(c >= LENT)
+        def _():
+            natural_step(3, c, False)
+
+        @pl.when(not_diag & (c < LENT))
         def _():
             got(rowp, rrecv, lent, c)
+
     over(last)
     multiply(lent)
 
@@ -308,6 +350,10 @@
             plane_step(k, c, True)
         for u in range(3):
             line_step(u, c, True)
+
+        @pl.when(c >= LENT)
+        def _():
+            natural_step(3, c, True)
     over(drain)
 
 

time: 42.5 us -> 39.3 us (0.925)
  Pallas kernels: 39.6 us -> 36.1 us
    pallas_call x1, Pallas kernels: 39.6 us -> 36.1 us  [fused(): pl.pallas_call(gram_kernel, out_shape=(half, half), in_specs=[hbm] * 4, o...]
where the time goes in v4:
time: 39.3 us; the launch traced here: 38.9 us
  Pallas kernels  36.1 us (92%)
  other arithmetic  2.78 us (7%)
    pallas_call x1, Pallas kernels, fused(): pl.pallas_call(gram_kernel, out_shape=(half, half), in_specs=[hbm] * 4, o...  36.1 us
    add x1, other arithmetic, fused(): return (mine + other).reshape(2 * width, full)  2.78 us

profile of v4, /device:TPU:6, one launch (start us, length us, event | category | flops | bytes accessed | tf_op | source)
XLA Modules:
  0.0 38.9 jit_solution(11881489364667801017)
XLA Ops:
  0.0 36.1 %shard_map.46 = (f32[2,192,768]{2,1,0:T(8,128)}, f32[2,192,768]{2,1,0:T(8,128)}) custom-call(bf16[192,1024]{1,0:T(8,128)(2,1)} %bitcast.2, s32[1,192]{1,0:T(1,128)} %slot_in.1, f32[1024]{0:T(1024)} %weight_in.1, s32[1,4]{1,0:T(1,128)} %valid_in.1), custom_call_target="tpu_custom_call" | custom-call | flops 905969664 | bytes 8388608 | tf_op jit(solution)/shard_map/pallas_call | solution.py:370
  36.1 2.8 %add.3 = f32[2,192,768]{2,1,0:T(8,128)} add(f32[2,192,768]{2,1,0:T(8,128)} %get-tuple-element.7, f32[2,192,768]{2,1,0:T(8,128)} %get-tuple-element.8) | non-fusion elementwise | flops 294912 | bytes 3538944 | tf_op jit(solution)/shard_map/add | solution.py:395

commit v5 on v4

--- a/solution.py
+++ b/solution.py
@@ -386,12 +386,12 @@
             dma((1,)), grid4, grid4, grid4, grid4, grid4, grid4, grid4, dma((2,)), dma((2,)), dma((2,)),
         ],
         compiler_params=pltpu.CompilerParams(
-            collective_id=0, has_side_effects=True, vmem_limit_bytes=63 * 2**20
+            collective_id=0, has_side_effects=True, vmem_limit_bytes=48 * 2**20
         ),
         cost_estimate=pl.CostEstimate(
             flops=2 * full * full * kept, bytes_accessed=8 * 2**20, transcendentals=0
         ),
-    )(snapshots.T, slot_map, row_weight, valid_rows)
+    )(*(pltpu.with_memory_space_constraint(x, pltpu.HBM) for x in (snapshots.T, slot_map, row_weight, valid_rows)))
     return (mine + other).reshape(2 * width, full)
 
 

time: 39.3 us -> 37.5 us (0.954)
  other arithmetic: 2.78 us -> 1.15 us
    add x1, other arithmetic: 2.78 us -> 1.15 us  [fused(): return (mine + other).reshape(2 * width, full)]
where the time goes in v5:
time: 37.5 us; the launch traced here: 37 us
  Pallas kernels  35.8 us (95%)
  other arithmetic  1.15 us (3%)
    pallas_call x1, Pallas kernels, fused(): pl.pallas_call(gram_kernel, out_shape=(half, half), in_specs=[hbm] * 4, o...  35.8 us
    add x1, other arithmetic, fused(): return (mine + other).reshape(2 * width, full)  1.15 us

profile of v5, /device:TPU:6, one launch (start us, length us, event | category | flops | bytes accessed | tf_op | source)
XLA Modules:
  0.0 37.0 jit_solution(15653112950051933171)
XLA Ops:
  0.0 35.8 %shard_map.46 = (f32[2,192,768]{2,1,0:T(8,128)S(1)}, f32[2,192,768]{2,1,0:T(8,128)S(1)}) custom-call(bf16[192,1024]{1,0:T(8,128)(2,1)} %bitcast.2, s32[1,192]{1,0:T(1,128)} %slot_in.1, f32[1024]{0:T(1024)} %weight_in.1, s32[1,4]{1,0:T(1,128)} %valid_in.1), custom_call_target="tpu_custom_call" | custom-call | flops 905969664 | bytes 8388608 | tf_op jit(solution)/shard_map/pallas_call | solution.py:370
  35.8 1.1 %add.3 = f32[2,192,768]{2,1,0:T(8,128)} add(f32[2,192,768]{2,1,0:T(8,128)S(1)} %get-tuple-element.7, f32[2,192,768]{2,1,0:T(8,128)S(1)} %get-tuple-element.8) | non-fusion elementwise | flops 294912 | bytes 3538944 | tf_op jit(solution)/shard_map/add | solution.py:395

commit v6 on v5

--- a/solution.py
+++ b/solution.py
@@ -6,8 +6,8 @@
 from jax.sharding import PartitionSpec as P
 
 MESH = pl.DeviceIdType.MESH
-CHUNKS = 3
-LENT = 3
+CHUNKS = 4
+LENT = 4
 
 
 def nt(a, b):

time: 37.5 us -> 36.6 us (0.976)
  Pallas kernels: 35.8 us -> 34.8 us
    pallas_call x1, Pallas kernels: 35.8 us -> 34.8 us  [fused(): pl.pallas_call(gram_kernel, out_shape=(half, half), in_specs=[hbm] * 4, o...]
where the time goes in v6:
time: 36.6 us; the launch traced here: 35.9 us
  Pallas kernels  34.8 us (95%)
  other arithmetic  1.15 us (3%)
    pallas_call x1, Pallas kernels, fused(): pl.pallas_call(gram_kernel, out_shape=(half, half), in_specs=[hbm] * 4, o...  34.8 us
    add x1, other arithmetic, fused(): return (mine + other).reshape(2 * width, full)  1.15 us

profile of v6, /device:TPU:6, one launch (start us, length us, event | category | flops | bytes accessed | tf_op | source)
XLA Modules:
  0.0 35.9 jit_solution(7494580707379892696)
XLA Ops:
  0.0 34.8 %shard_map.46 = (f32[2,192,768]{2,1,0:T(8,128)S(1)}, f32[2,192,768]{2,1,0:T(8,128)S(1)}) custom-call(bf16[192,1024]{1,0:T(8,128)(2,1)} %bitcast.2, s32[1,192]{1,0:T(1,128)} %slot_in.1, f32[1024]{0:T(1024)} %weight_in.1, s32[1,4]{1,0:T(1,128)} %valid_in.1), custom_call_target="tpu_custom_call" | custom-call | flops 905969664 | bytes 8388608 | tf_op jit(solution)/shard_map/pallas_call | solution.py:370
  34.8 1.1 %add.3 = f32[2,192,768]{2,1,0:T(8,128)} add(f32[2,192,768]{2,1,0:T(8,128)S(1)} %get-tuple-element.7, f32[2,192,768]{2,1,0:T(8,128)S(1)} %get-tuple-element.8) | non-fusion elementwise | flops 294912 | bytes 3538944 | tf_op jit(solution)/shard_map/add | solution.py:395
